TPU v7x, 512 devices: a whole 4x8x8 slice. The times are simulated.
512 devices in a mesh: col: 8 (over x, core), row: 64 (over z, y).
Axes of the slice: x: 4, y: 8, z: 8, core: 2. Of those that a mesh axis runs over, the one named last changes fastest.
Arguments:
- weight_delta: bfloat16 [7168, 32768], P('col', 'row'), may hold values from -96 to 96, as said below
Outputs:
- orthogonalized: bfloat16 [7168, 32768], P('col', 'row')
Inputs may be any that keep to these rules, and one draw needn't show every extreme that they name: `weight_delta`: every entry is finite.
All inputs are finite; a program needn't handle non-finite values. Where the computation divides by a largest or mean magnitude, that divisor is 1e-20 or more.
Results may differ from a plain program's by a relative error of at most 0.0012.
The roundings to bfloat16 on the way count: a program that leaves them out, or rounds other values in their place, can miss the bound.
Values may be sent and summed in bfloat16 or wider, within the bound.
A program may use at most 128 MiB of HBM per device.

v0:
```python
import jax
import jax.numpy as jnp
from jax import lax
from jax.sharding import PartitionSpec as P

BLOCK = 112
MEETINGS = 2
NS_STEPS = 2


eps_value = 1e-06


def extended_2(shard, sides, width):
    for axis, dim in sides:
        size, length = (lax.axis_size(axis), shard.shape[dim])
        up = [(i, (i + 1) % size) for i in range(size - 1)]
        down = [(j, i) for i, j in up]
        last = lax.slice_in_dim(shard, length - width, length, axis=dim)
        leading = lax.slice_in_dim(shard, 0, width, axis=dim)
        before = lax.ppermute(last, axis, up)
        after = lax.ppermute(leading, axis, down)
        shard = jnp.concatenate([before, shard, after], axis=dim)
    return shard


def rotation(gram):
    pair_width = gram.shape[0]
    identity = jnp.eye(pair_width, dtype=jnp.float32)
    diagonal = jnp.diagonal(gram)
    inverse = lax.rsqrt(diagonal + eps_value)
    norm_root = jnp.sqrt(diagonal + eps_value)
    normed = gram * inverse[:, None] * inverse[None, :]
    row_bound = jnp.max(jnp.sum(jnp.abs(normed), axis=1))
    upper = normed / row_bound
    factor = identity
    for iteration in range(NS_STEPS):
        middle = 1.5 * identity - 0.5 * jnp.dot(factor, upper, precision=lax.Precision.HIGHEST)
        upper = jnp.dot(upper, middle, precision=lax.Precision.HIGHEST)
        factor = jnp.dot(middle, factor, precision=lax.Precision.HIGHEST)
    turning = inverse[:, None] * factor * norm_root[None, :] / jnp.sqrt(row_bound)
    return turning.astype(jnp.bfloat16)


def pair_products(left_rows, right_rows):
    return jnp.einsum("pak,pbk->pab", left_rows, right_rows, preferred_element_type=jnp.float32)


def summed_grams(stacked):
    return lax.psum(pair_products(stacked, stacked), "row")


def pair_updates(blocks, resting_mask, block_width):
    row_count = blocks.shape[1]
    stacked = blocks.reshape(-1, 2 * block_width, row_count)
    gram = summed_grams(stacked)
    identity = jnp.eye(2 * block_width, dtype=jnp.float32)
    gram = jnp.where(resting_mask[:, None, None], identity[None], gram)
    turning = jax.vmap(rotation)(gram)
    updated = jnp.einsum("pab,par->pbr", turning, stacked, preferred_element_type=jnp.float32)
    updated = updated.astype(jnp.bfloat16)
    traded = jnp.concatenate([updated[:, block_width:], updated[:, :block_width]], axis=1)
    return traded.reshape(-1, row_count)


def shards(weight_delta):
    block_width = BLOCK
    local_pairs = weight_delta.shape[0] // (2 * block_width)
    position = lax.axis_index("col")
    col_count = lax.axis_size("col")
    is_first = position == 0
    is_last = position == col_count - 1
    current = weight_delta
    for meeting in range(MEETINGS):
        if meeting % 2 == 0:
            current = pair_updates(current, jnp.zeros((local_pairs,), bool), block_width)
        else:
            extended = extended_2(current, (("col", 0),), block_width)
            resting_mask = (
                jnp.zeros((local_pairs + 1,), bool).at[0].set(is_first).at[local_pairs].set(is_last)
            )
            renewed = pair_updates(extended, resting_mask, block_width)[block_width:-block_width]
            first_block = jnp.where(is_first, current[:block_width], renewed[:block_width])
            last_block = jnp.where(is_last, current[-block_width:], renewed[-block_width:])
            current = jnp.concatenate(
                [first_block, renewed[block_width:-block_width], last_block], axis=0
            )
    return current


def solution(mesh):
    placed = (P("col", "row"),)
    return jax.shard_map(
        shards, mesh=mesh, in_specs=placed, out_specs=P("col", "row"), check_vma=False
    )
```

profile of v0, /device:TPU:1, one launch (start us, length us, event | category | flops | bytes accessed | tf_op | source)
XLA Modules:
  0.0 402.5 jit_solution(3634650118063269475)
XLA Ops:
  6.5 1.2 copy-done
  7.7 1.3 fusion.33
  9.2 162.8 %all-reduce.4.cloned.1.call-done = f32[4,224,224]{2,1,0:T(8,128)} async-done(((f32[4,224,224]{2,1,0:T(8,128)}), f32[4,224,224]{2,1,0:T(8,128)}) %all-reduce.4.cloned.1.call-update) | async-done | bytes 802832 | tf_op jit(solution)/shard_map/psum | solution.py:50
  172.0 13.6 %copy.22 = f32[4,224,224]{0,2,1:T(8,128)} copy(f32[4,224,224]{2,1,0:T(8,128)} %all-reduce.4.cloned.1.call-done) | data formatting | bytes 1605632 | tf_op jit(solution)/shard_map/psum | solution.py:50
  185.5 3.7 gather_fusion
  189.4 0.4 abs_reduce_fusion.1
  189.8 0.1 reduce_max.18
  189.9 0.8 fusion.9
  190.7 0.6 fusion.21
  191.3 1.1 fusion.27
  192.4 1.0 fusion.7
  193.5 1.1 fusion.11
  194.6 0.5 convolution_convert_fusion.1
  195.3 7.6 %collective-permute-start = (bf16[112,512]{1,0:T(8,128)(2,1)S(1)}, bf16[112,512]{1,0:T(8,128)(2,1)S(1)}, u32[]{:S(2)}, u32[]{:S(2)}) collective-permute-start(bf16[112,512]{1,0:T(8,128)(2,1)S(1)} %get-tuple-element.33), channel_id=1, source_target_pairs={{0,64},{64,128},{128,192},{192,256},{256,320},{320,384},{384,448},... | collective-permute-start | bytes 344072 | tf_op jit(solution)/shard_map/ppermute | solution.py:21
  202.8 1.9 collective-permute-start.1
  204.8 4.2 %collective-permute-done.1 = bf16[112,512]{1,0:T(8,128)(2,1)S(1)} collective-permute-done((bf16[112,512]{1,0:T(8,128)(2,1)S(1)}, bf16[112,512]{1,0:T(8,128)(2,1)S(1)}, u32[]{:S(2)}, u32[]{:S(2)}) %collective-permute-start.1) | collective-permute-done | bytes 114720 | tf_op jit(solution)/shard_map/ppermute | solution.py:22
  209.0 1.5 fusion.34
  210.5 0.2 scatter.9
  210.8 150.1 %all-reduce.6.cloned.1.call-done = f32[5,224,224]{2,1,0:T(8,128)} async-done(((f32[5,224,224]{2,1,0:T(8,128)}), f32[5,224,224]{2,1,0:T(8,128)}) %all-reduce.6.cloned.1.call-update) | async-done | bytes 1003536 | tf_op jit(solution)/shard_map/psum | solution.py:50
  360.9 2.4 broadcast_select_fusion
  363.3 13.5 %copy.27 = f32[5,224,224]{0,2,1:T(8,128)} copy(f32[5,224,224]{2,1,0:T(8,128)} %broadcast_select_fusion) | data formatting | bytes 2007040 | tf_op jit(solution)/shard_map/jit(_where)/select_n | solution.py:58
  376.8 3.7 gather_fusion.1
  380.6 1.8 abs_reduce_fusion
  382.4 0.1 reduce_max.19
  382.5 2.3 fusion.1
  384.8 2.4 fusion.24
  387.2 1.7 fusion.18
  389.0 3.0 fusion.4
  392.0 1.3 fusion.10
  393.3 0.6 convolution_convert_fusion
  394.2 1.0 pad_maximum_fusion.3
  395.1 0.5 copy-done.1
  (33 shorter events, 1.0 us)
Async XLA Ops:
  6.5 1.2 copy-start
  6.5 165.4 %all-reduce.4.cloned.1.call-start = ((), (), s32[]{:S(2)}) async-start(), calls=%async_computation | async-start | bytes 1835008 | tf_op jit(solution)/shard_map/psum | solution.py:50
  9.1 351.8 %all-reduce.6.cloned.1.call-start = ((), (), s32[]{:S(2)}) async-start(), calls=%async_computation.1 | async-start | bytes 2293760 | tf_op jit(solution)/shard_map/psum | solution.py:50
  172.0 17.4 %copy-start.4 = (f32[4,224,224]{2,1,0:T(8,128)S(1)}, f32[4,224,224]{2,1,0:T(8,128)}, u32[]{:S(2)}) copy-start(f32[4,224,224]{2,1,0:T(8,128)} %all-reduce.4.cloned.1.call-done) | copy-start | bytes 2408452
  195.3 9.5 %collective-permute-start = (bf16[112,512]{1,0:T(8,128)(2,1)S(1)}, bf16[112,512]{1,0:T(8,128)(2,1)S(1)}, u32[]{:S(2)}, u32[]{:S(2)}) collective-permute-start(bf16[112,512]{1,0:T(8,128)(2,1)S(1)} %get-tuple-element.33), channel_id=1, source_target_pairs={{0,64},{64,128},{128,192},{192,256},{256,320},{320,384},{384,448},... | collective-permute-start | bytes 344072 | tf_op jit(solution)/shard_map/ppermute | solution.py:21
  202.8 6.1 %collective-permute-start.1 = (bf16[112,512]{1,0:T(8,128)(2,1)S(1)}, bf16[112,512]{1,0:T(8,128)(2,1)S(1)}, u32[]{:S(2)}, u32[]{:S(2)}) collective-permute-start(bf16[112,512]{1,0:T(8,128)(2,1)S(1)} %get-tuple-element.34), channel_id=1, source_target_pairs={{64,0},{128,64},{192,128},{256,192},{320,256},{384,320},{448,384},... | collective-permute-start | bytes 344072 | tf_op jit(solution)/shard_map/ppermute | solution.py:22
  382.5 2.3 copy-start.2
  389.0 3.0 copy-start.3
  394.1 1.5 copy-start.1
Sparse Core Ops, SparseCore 0:
  10.6 161.3 all-reduce.3
  210.6 150.1 all-reduce.5
where the time goes:
time: 406 us; the launch traced here: 402 us
  waiting for transfers between devices  317 us (78%)
  local copies, waits for them, and re-layouts  36.8 us (9%)
  matrix products  19.2 us (5%)
  between operations  13.7 us (3%)
  starting transfers between devices  9.52 us (2%)
  other arithmetic  6.26 us (2%)
    psum x2, waiting for transfers between devices, summed_grams(): return lax.psum(pair_products(stacked, stacked), 'row')  313 us
    psum x1, local copies, waits for them, and re-layouts, summed_grams(): return lax.psum(pair_products(stacked, stacked), 'row')  13.6 us
    select_n x1, local copies, waits for them, and re-layouts, pair_updates(): gram = jnp.where(resting_mask[:, None, None], identity[None], gram)  13.5 us
  transfers between devices with their start and end apart: 4, of which 3 were waited for; matrix products, arithmetic and copies ran while one was open for 0% of the time, Pallas kernels for 0%

commit v1 on v0

v1 whole, which is shorter than its diff:
```python
import functools

import jax
import jax.numpy as jnp
from jax import lax
from jax.experimental import pallas as pl
from jax.experimental.pallas import tpu as pltpu
from jax.sharding import PartitionSpec as P

BLOCK = 112
PAD = 128
PAIRS = 4
SIDE = 8
CHUNK = 56
GROUPS = 3
EPS = 1e-6
MESH = pl.DeviceIdType.MESH
FAR_FIRST = (4, 3, 5, 2, 6, 1, 7)


def dot(a, b):
    return jnp.dot(a, b, preferred_element_type=jnp.float32)


def dot_nt(a, b):
    return lax.dot_general(a, b, (((1,), (1,)), ((), ())), preferred_element_type=jnp.float32)


def halves(x):
    high = x.astype(jnp.bfloat16)
    low = (x - high.astype(jnp.float32)).astype(jnp.bfloat16)
    return high, low


def dot3(a, b):
    a_high, a_low = a
    b_high, b_low = b
    return dot(a_high, b_high) + (dot(a_high, b_low) + dot(a_low, b_high))


def both_sides(left, x, right):
    high, low = halves(x)
    high, low = halves(dot(left, high) + dot(left, low))
    return dot_nt(high, right) + dot_nt(low, right)


def turning_transposed(gram):
    shape = gram.shape
    eye = lax.broadcasted_iota(jnp.int32, shape, 0) == lax.broadcasted_iota(jnp.int32, shape, 1)
    diagonals = jnp.where(eye, gram, 0.0)
    down = jnp.sum(diagonals, axis=1, keepdims=True) + EPS
    across = jnp.sum(diagonals, axis=0, keepdims=True) + EPS
    inverse_across = lax.rsqrt(across)
    normed = gram * lax.rsqrt(down) * inverse_across
    bound = jnp.max(jnp.sum(jnp.abs(normed), axis=0, keepdims=True), axis=1, keepdims=True)
    upper = normed * (1.0 / bound)
    parts = halves(upper)
    square = dot3(parts, parts)
    rest = dot3(halves(square), halves(-0.5625 * upper + 0.0625 * square))
    factor = jnp.where(eye, 2.25, 0.0) - 2.4375 * upper + 1.6875 * square + rest
    return (factor * (jnp.sqrt(down) * lax.rsqrt(bound)) * inverse_across).astype(jnp.bfloat16)


def tile_iotas():
    return (
        lax.broadcasted_iota(jnp.int32, (PAD, PAD), 0),
        lax.broadcasted_iota(jnp.int32, (PAD, PAD), 1),
    )


def packed(first, last):
    row, column = tile_iotas()
    turned = pltpu.roll(last, PAD - 1, 1)
    return jnp.where((column < row) | (column == PAD - 1), turned, first)[:BLOCK]


def padded(x):
    return jnp.concatenate([x, jnp.zeros((PAD - BLOCK, PAD), jnp.float32)], axis=0)


def unpacked(both):
    row, column = tile_iotas()
    both = padded(both)
    first = jnp.where((column >= row) & (column < BLOCK), both, 0.0)
    first = jnp.where(column >= row, first, first.T)
    last = jnp.where(column <= row, pltpu.roll(both, 1, 1), 0.0)
    last = jnp.where(column <= row, last, last.T)
    return first, last


def square_of(a, b, c, d):
    return jnp.concatenate([jnp.concatenate([a, b], axis=1), jnp.concatenate([c, d], axis=1)], axis=0)


def kernel(
    x_ref, o_ref, own, beside, part, gathered, middle, full, grams, turn, stack, corner, corner_in, turn_in, wide, wide_in,
    staged, in_sem, out_sem, send_sem, recv_sem, side_send, side_recv,
):
    c, r = lax.axis_index("col"), lax.axis_index("row")
    col_count = lax.axis_size("col")
    z, y = lax.div(r, SIDE), lax.rem(r, SIDE)
    left, right = (lax.rem(c + col_count - 1, col_count), r), (lax.rem(c + 1, col_count), r)

    def along_y(step):
        return (c, z * SIDE + lax.rem(y + step, SIDE))

    def along_z(step):
        return (c, lax.rem(z + step, SIDE) * SIDE + y)

    places = ((y, z), (z, y))
    movers = ((along_y, along_z), (along_z, along_y))

    barrier = pltpu.get_barrier_semaphore()
    for step in range(1, SIDE):
        pl.semaphore_signal(barrier, inc=1, device_id=along_y(step), device_id_type=MESH)
        pl.semaphore_signal(barrier, inc=1, device_id=along_z(step), device_id_type=MESH)
    for side in (left, right):
        pl.semaphore_signal(barrier, inc=1, device_id=side, device_id_type=MESH)

    loads = []
    for b in range(2 * PAIRS):
        loads.append(
            pltpu.make_async_copy(
                x_ref.at[pl.ds(b * BLOCK, BLOCK)], own.at[b // 2, pl.ds((b % 2) * PAD, BLOCK)], in_sem.at[b]
            )
        )
        loads[-1].start()
    gap = jnp.zeros((PAD - BLOCK, own.shape[-1]), jnp.bfloat16)
    for lower in (BLOCK, PAD + BLOCK):
        beside[pl.ds(lower, PAD - BLOCK)] = gap
        for k in range(PAIRS):
            own[k, pl.ds(lower, PAD - BLOCK)] = gap

    def sideways(source, target, index, device):
        return pltpu.make_async_remote_copy(
            src_ref=source, dst_ref=target, send_sem=side_send.at[index], recv_sem=side_recv.at[index],
            device_id=device, device_id_type=MESH,
        )

    pair_out = [
        sideways(x_ref.at[pl.ds(b * BLOCK, BLOCK)], beside.at[pl.ds(b * PAD, BLOCK)], b, left) for b in range(2)
    ]
    turn_out = sideways(turn.at[0, pl.ds(PAD, PAD)], turn_in, 2, left)
    corner_out = sideways(corner, corner_in, 3, left)
    block_out = sideways(stack.at[PAIRS, pl.ds(0, PAD)], stack.at[0, pl.ds(0, PAD)], 4, right)
    wide_out = sideways(wide, wide_in, 5, right)

    pl.semaphore_wait(barrier, 2 * (SIDE - 1) + 2)
    for copy in pair_out:
        copy.start()

    def send(group, half, phase, source_of, target):
        mover = movers[half][1 if phase == 1 else 0]
        for step in FAR_FIRST:
            device = mover(step)
            pltpu.make_async_remote_copy(
                src_ref=source_of(step), dst_ref=target,
                send_sem=send_sem.at[group, half, phase], recv_sem=recv_sem.at[group, half, phase],
                device_id=device, device_id_type=MESH,
            ).start()

    def wait(sem, group, half, phase):
        seven = gathered.at[group, half, pl.ds(0, SIDE - 1)]
        pltpu.make_async_copy(seven, seven, sem.at[group, half, phase]).wait()

    def spread(group, half):
        place = places[half][0]
        gathered[group, half, place] = part[group, half * SIDE + place]
        send(
            group, half, 0,
            lambda step: part.at[group, half * SIDE + lax.rem(place + step, SIDE)],
            gathered.at[group, half, place],
        )

    def summed(ref, group, half):
        total = ref[group, half, 0]
        for i in range(1, SIDE):
            total = total + ref[group, half, i]
        return total

    def cross(group, half):
        wait(recv_sem, group, half, 0)
        place = places[half][1]
        middle[group, half, place] = summed(gathered, group, half)
        here = middle.at[group, half, place]
        send(group, half, 1, lambda step: here, here)

    def share(group, half):
        wait(recv_sem, group, half, 1)
        place = half * SIDE + places[half][0]
        full[group, place] = summed(middle, group, half)
        here = full.at[group, place]
        send(group, half, 2, lambda step: here, here)

    def put(group, chunk, x):
        part[group, pl.ds(chunk, 2)] = x[:BLOCK].reshape(2, CHUNK, PAD)

    def take(group, chunk):
        return full[group, pl.ds(chunk, 2)].reshape(BLOCK, PAD)

    for k in range(PAIRS):
        loads[2 * k].wait()
        loads[2 * k + 1].wait()
        pair = own[k]
        gram = dot_nt(pair, pair)
        put(0, 4 * k, packed(gram[:PAD, :PAD], gram[PAD:, PAD:]))
        put(0, 4 * k + 2, gram[:PAD, PAD:])
        if k % 2 == 1:
            spread(0, k // 2)
    for k in range(PAIRS):
        group, half = 1 + k // 2, k % 2
        if k == PAIRS - 1:
            for copy in pair_out:
                copy.wait_recv()
        cross_gram = dot_nt(own[k], own[k + 1] if k < PAIRS - 1 else beside[...])
        put(group, half * SIDE, cross_gram[:PAD, :PAD])
        put(group, half * SIDE + 2, cross_gram[:PAD, PAD:])
        put(group, half * SIDE + 4, cross_gram[PAD:, :PAD])
        put(group, half * SIDE + 6, cross_gram[PAD:, PAD:])
        spread(group, half)
    for group in range(GROUPS):
        for half in range(2):
            cross(group, half)
    for group in range(GROUPS):
        for half in range(2):
            share(group, half)

    for half in range(2):
        wait(recv_sem, 0, half, 2)
    for k in range(PAIRS):
        first, last = unpacked(take(0, 4 * k))
        between = padded(take(0, 4 * k + 2))
        grams[k] = square_of(first, between, between.T, last)
    for k in range(PAIRS):
        turn[k] = turning_transposed(grams[k])
    turn_out.start()
    for k in (PAIRS - 1, 0, 1, 2):
        updated = dot(turn[k], own[k]).astype(jnp.bfloat16)
        stack[k + 1, pl.ds(0, PAD)] = updated[:PAD]
        stack[k, pl.ds(PAD, PAD)] = updated[PAD:]
        if k == PAIRS - 1:
            block_out.start()
    firsts, lasts = [], []
    for k in range(PAIRS):
        firsts.append(both_sides(turn[k, pl.ds(0, PAD)], grams[k], turn[k, pl.ds(0, PAD)]))
        lasts.append(both_sides(turn[k, pl.ds(PAD, PAD)], grams[k], turn[k, pl.ds(PAD, PAD)]))
        if k == 0:
            corner[...] = lasts[0]
            corner_out.start()
    turn_out.wait_recv()
    stack[PAIRS, pl.ds(PAD, PAD)] = dot(turn_in[...], beside[...]).astype(jnp.bfloat16)

    stores = [
        pltpu.make_async_copy(staged.at[b], o_ref.at[pl.ds(b * BLOCK, BLOCK)], out_sem.at[b]) for b in range(2 * PAIRS)
    ]

    def second(k):
        group, half = 1 + k // 2, k % 2
        quarters = [padded(take(group, half * SIDE + 2 * i)) for i in range(4)]
        inner = k < PAIRS - 1
        other = turn[k + 1, pl.ds(PAD, PAD)] if inner else turn_in[...]
        between = both_sides(turn[k, pl.ds(0, PAD)], square_of(*quarters), other)
        last = lasts[k + 1] if inner else corner_in[...]
        return turning_transposed(square_of(firsts[k], between, between.T, last))

    def finish(k, turning):
        updated = dot(turning, stack[k + 1]).astype(jnp.bfloat16)
        staged[2 * k + 1] = updated[PAD : PAD + BLOCK]
        if k < PAIRS - 1:
            staged[2 * k + 2] = updated[:BLOCK]
            stores[2 * k + 2].start()
        else:
            staged[2 * k + 1] = jnp.where(c == col_count - 1, stack[PAIRS, pl.ds(0, BLOCK)], updated[PAD : PAD + BLOCK])
        stores[2 * k + 1].start()

    for half in range(2):
        wait(recv_sem, 1, half, 2)
    for k, turning in enumerate([second(0), second(1)]):
        finish(k, turning)
    for half in range(2):
        wait(recv_sem, 2, half, 2)
    corner_out.wait_recv()
    turning = second(PAIRS - 1)
    wide[...] = turning[:PAD]
    wide_out.start()
    finish(PAIRS - 1, turning)
    finish(2, second(2))
    block_out.wait_recv()
    wide_out.wait_recv()
    first_block = dot(wide_in[...], stack[0]).astype(jnp.bfloat16)[:BLOCK]
    staged[0] = jnp.where(c == 0, stack[0, pl.ds(PAD, BLOCK)], first_block)
    stores[0].start()

    for copy in pair_out + [turn_out, corner_out, block_out, wide_out]:
        copy.wait_send()
    for group in range(GROUPS):
        for half in range(2):
            for phase in range(3):
                wait(send_sem, group, half, phase)
    for copy in stores:
        copy.wait()


def shards(weight_delta):
    width = weight_delta.shape[1]
    chunks = (GROUPS, 2, SIDE, CHUNK, PAD)
    whole = (GROUPS, 2 * SIDE, CHUNK, PAD)
    f32, bf16 = jnp.float32, jnp.bfloat16
    return pl.pallas_call(
        kernel,
        out_shape=jax.ShapeDtypeStruct(weight_delta.shape, bf16),
        in_specs=[pl.BlockSpec(memory_space=pl.ANY)],
        out_specs=pl.BlockSpec(memory_space=pl.ANY),
        scratch_shapes=[
            pltpu.VMEM((PAIRS, 2 * PAD, width), bf16),
            pltpu.VMEM((2 * PAD, width), bf16),
            pltpu.VMEM(whole, f32),
            pltpu.VMEM(chunks, f32),
            pltpu.VMEM(chunks, f32),
            pltpu.VMEM(whole, f32),
            pltpu.VMEM((PAIRS, 2 * PAD, 2 * PAD), f32),
            pltpu.VMEM((PAIRS, 2 * PAD, 2 * PAD), bf16),
            pltpu.VMEM((PAIRS + 1, 2 * PAD, width), bf16),
            pltpu.VMEM((PAD, PAD), f32),
            pltpu.VMEM((PAD, PAD), f32),
            pltpu.VMEM((PAD, 2 * PAD), bf16),
            pltpu.VMEM((PAD, 2 * PAD), bf16),
            pltpu.VMEM((PAD, 2 * PAD), bf16),
            pltpu.VMEM((2 * PAIRS, BLOCK, width), bf16),
            pltpu.SemaphoreType.DMA((2 * PAIRS,)),
            pltpu.SemaphoreType.DMA((2 * PAIRS,)),
            pltpu.SemaphoreType.DMA((GROUPS, 2, 3)),
            pltpu.SemaphoreType.DMA((GROUPS, 2, 3)),
            pltpu.SemaphoreType.DMA((6,)),
            pltpu.SemaphoreType.DMA((6,)),
        ],
        compiler_params=pltpu.CompilerParams(
            collective_id=0, has_side_effects=True, vmem_limit_bytes=40 * 2**20
        ),
    )(weight_delta)


def solution(mesh):
    return jax.shard_map(
        shards, mesh=mesh, in_specs=(P("col", "row"),), out_specs=P("col", "row"), check_vma=False
    )
```

time: 406 us -> 70.2 us (0.17)
  waiting for transfers between devices: 317 us -> 0 us
  Pallas kernels: 0 us -> 68 us
  local copies, waits for them, and re-layouts: 36.8 us -> 2.1 us
  matrix products: 19.2 us -> 0 us
  between operations: 13.7 us -> 0.01 us
  starting transfers between devices: 9.52 us -> 0 us
  other arithmetic: 6.26 us -> 0 us
    psum x2 -> x0, waiting for transfers between devices: 313 us -> none  [summed_grams(): return lax.psum(pair_products(stacked, stacked), 'row')]
    pallas_call x0 -> x1, Pallas kernels: none -> 68 us  [shards(): pl.pallas_call(kernel, out_shape=jax.ShapeDtypeStruct(weight_delta.shape,...]
    dot_general x14 -> x0, matrix products: 19.2 us -> none  [the longest x4 7.11 us: rotation(): jnp.dot(factor, upper, precision=lax.Precision.HIGHEST)]
    psum x1 -> x0, local copies, waits for them, and re-layouts: 13.6 us -> none  [summed_grams(): return lax.psum(pair_products(stacked, stacked), 'row')]
    select_n x1 -> x0, local copies, waits for them, and re-layouts: 13.5 us -> none  [pair_updates(): gram = jnp.where(resting_mask[:, None, None], identity[None], gram)]
    ppermute x2 -> x0, starting transfers between devices: 9.47 us -> none  [the longest x1 7.55 us: extended_2(): before = lax.ppermute(last, axis, up)]
    gather x2 -> x0, local copies, waits for them, and re-layouts: 7.35 us -> none  [rotation(): diagonal = jnp.diagonal(gram)]
    ppermute x2 -> x0, waiting for transfers between devices: 4.17 us -> none  [the longest x1 4.17 us: extended_2(): after = lax.ppermute(leading, axis, down)]
  transfers between devices with their start and end apart: 4 -> 0, of which waited for: 3 -> 0; matrix products, arithmetic and copies ran while one was open for 0% -> 0% of each run, Pallas kernels for 0% -> 0%
where the time goes in v1:
time: 70.2 us; the launch traced here: 70.1 us
  Pallas kernels  68 us (97%)
  local copies, waits for them, and re-layouts  2.1 us (3%)
    pallas_call x1, Pallas kernels, shards(): pl.pallas_call(kernel, out_shape=jax.ShapeDtypeStruct(weight_delta.shape,...  68 us
    unnamed x3, local copies, waits for them, and re-layouts  2.1 us

profile of v1, /device:TPU:1, one launch (start us, length us, event | category | flops | bytes accessed | tf_op | source)
XLA Modules:
  0.0 70.1 jit_solution(3372586009064132622)
XLA Ops:
  0.0 0.0 copy-start
  0.0 1.2 %copy-done = bf16[896,512]{1,0:T(8,128)(2,1)S(1)} copy-done((bf16[896,512]{1,0:T(8,128)(2,1)S(1)}, bf16[896,512]{1,0:T(8,128)(2,1)}, u32[]{:S(2)}) %copy-start) | copy-done | bytes 917528
  1.2 68.0 %shard_map.17 = bf16[896,512]{1,0:T(8,128)(2,1)S(1)} custom-call(bf16[896,512]{1,0:T(8,128)(2,1)S(1)} %copy-done), custom_call_target="tpu_custom_call" | custom-call | tf_op jit(solution)/shard_map/pallas_call | solution.py:309
  69.2 0.9 %copy.3 = bf16[896,512]{1,0:T(8,128)(2,1)} copy(bf16[896,512]{1,0:T(8,128)(2,1)S(1)} %shard_map.17) | data formatting | bytes 1835008
Async XLA Ops:
  0.0 1.2 %copy-start = (bf16[896,512]{1,0:T(8,128)(2,1)S(1)}, bf16[896,512]{1,0:T(8,128)(2,1)}, u32[]{:S(2)}) copy-start(bf16[896,512]{1,0:T(8,128)(2,1)} %x_ref.1) | copy-start | bytes 2752516

commit v2 on v1

v2 whole, which is shorter than its diff:
```python
import functools

import jax
import jax.numpy as jnp
from jax import lax
from jax.experimental import pallas as pl
from jax.experimental.pallas import tpu as pltpu
from jax.sharding import PartitionSpec as P

BLOCK = 112
PAD = 128
PAIRS = 4
SIDE = 8
CHUNK = 56
TILE = 8
GROUPS = 3
EPS = 1e-6
STAGE, LAG, TURN = 10, 5, 60.5
CROSS_ORDER = (0, 3, 1, 2)
CROSS_PLACE = {0: (1, 0), 3: (1, 1), 1: (2, 0), 2: (2, 1)}
MESH = pl.DeviceIdType.MESH
FAR_FIRST = (4, 3, 5, 2, 6, 1, 7)


def dot(a, b):
    return jnp.dot(a, b, preferred_element_type=jnp.float32)


def dot_nt(a, b):
    return lax.dot_general(a, b, (((1,), (1,)), ((), ())), preferred_element_type=jnp.float32)


def halves(x):
    high = x.astype(jnp.bfloat16)
    low = (x - high.astype(jnp.float32)).astype(jnp.bfloat16)
    return high, low


def dot3(a, b):
    a_high, a_low = a
    b_high, b_low = b
    return dot(
        jnp.concatenate([a_high, a_high, a_low], axis=1), jnp.concatenate([b_high, b_low, b_high], axis=0)
    )


def both_sides(left, x, right):
    product = dot(jnp.concatenate([left, left], axis=1), jnp.concatenate(halves(x), axis=0))
    return dot_nt(jnp.concatenate(halves(product), axis=1), jnp.concatenate([right, right], axis=1))


def turning_transposed(gram):
    shape = gram.shape
    eye = lax.broadcasted_iota(jnp.int32, shape, 0) == lax.broadcasted_iota(jnp.int32, shape, 1)
    small_eye = eye[:PAD, :PAD]
    corners = [jnp.where(small_eye, gram[i : i + PAD, i : i + PAD], 0.0) for i in (0, PAD)]
    down = jnp.concatenate([jnp.sum(x, axis=1, keepdims=True) for x in corners], axis=0) + EPS
    across = jnp.concatenate([jnp.sum(x, axis=0, keepdims=True) for x in corners], axis=1) + EPS
    inverse_across = lax.rsqrt(across)
    normed = gram * lax.rsqrt(down) * inverse_across
    parts = halves(normed)
    square = dot3(parts, parts)
    bound = jnp.max(jnp.sum(jnp.abs(normed), axis=0, keepdims=True), axis=1, keepdims=True)
    share = 1.0 / bound
    share2 = share * share
    rest = dot3(halves(square), halves((-0.5625 * share * share2) * normed + (0.0625 * share2 * share2) * square))
    factor = jnp.where(eye, 2.25, 0.0) + (-2.4375 * share) * normed + (1.6875 * share2) * square + rest
    return (factor * (jnp.sqrt(down) * lax.rsqrt(bound)) * inverse_across).astype(jnp.bfloat16)


def tile_iotas():
    return (
        lax.broadcasted_iota(jnp.int32, (PAD, PAD), 0),
        lax.broadcasted_iota(jnp.int32, (PAD, PAD), 1),
    )


def packed(first, last):
    row, column = tile_iotas()
    turned = pltpu.roll(last, PAD - 1, 1)
    return jnp.where((column < row) | (column == PAD - 1), turned, first)[:BLOCK]


def padded(x):
    return jnp.concatenate([x, jnp.zeros((PAD - BLOCK, PAD), jnp.float32)], axis=0)


def unpacked(both):
    row, column = tile_iotas()
    both = padded(both)
    first = jnp.where((column >= row) & (column < BLOCK), both, 0.0)
    first = jnp.where(column >= row, first, first.T)
    last = jnp.where(column <= row, pltpu.roll(both, 1, 1), 0.0)
    last = jnp.where(column <= row, last, last.T)
    return first, last


def square_of(a, b, c, d):
    return jnp.concatenate([jnp.concatenate([a, b], axis=1), jnp.concatenate([c, d], axis=1)], axis=0)


def kernel(
    x_ref, o_ref, own, beside, part, relay_in, relay_out, final_in, middle, tiles, full, grams, turn, stack, corner,
    corner_in, turn_in, wide, wide_in, in_sem, send_sem, recv_sem, side_send, side_recv,
):
    c, r = lax.axis_index("col"), lax.axis_index("row")
    col_count = lax.axis_size("col")
    z, y = lax.div(r, SIDE), lax.rem(r, SIDE)
    left, right = (lax.rem(c + col_count - 1, col_count), r), (lax.rem(c + 1, col_count), r)
    tie = 2 * lax.rem(c, 2) - 1

    def ring(place, step):
        return lax.rem(place + step + SIDE, SIDE)

    def along_y(step):
        return (c, z * SIDE + ring(y, step))

    def along_z(step):
        return (c, ring(z, step) * SIDE + y)

    places = ((y, z), (z, y))
    movers = ((along_y, along_z), (along_z, along_y))

    barrier = pltpu.get_barrier_semaphore()
    for step in range(1, SIDE):
        pl.semaphore_signal(barrier, inc=1, device_id=along_y(step), device_id_type=MESH)
        pl.semaphore_signal(barrier, inc=1, device_id=along_z(step), device_id_type=MESH)
    for side in (left, right):
        pl.semaphore_signal(barrier, inc=1, device_id=side, device_id_type=MESH)

    loads = []
    for b in range(2 * PAIRS):
        loads.append(
            pltpu.make_async_copy(
                x_ref.at[pl.ds(b * BLOCK, BLOCK)], own.at[b // 2, pl.ds((b % 2) * PAD, BLOCK)], in_sem.at[b]
            )
        )
        loads[-1].start()
    gap = jnp.zeros((PAD - BLOCK, own.shape[-1]), jnp.bfloat16)
    for lower in (BLOCK, PAD + BLOCK):
        beside[pl.ds(lower, PAD - BLOCK)] = gap
        for k in range(PAIRS):
            own[k, pl.ds(lower, PAD - BLOCK)] = gap
    for group in range(GROUPS):
        for half in range(2):
            middle[group, half, SIDE - 1] = jnp.zeros((TILE, PAD), jnp.float32)

    def sideways(source, target, index, device):
        return pltpu.make_async_remote_copy(
            src_ref=source, dst_ref=target, send_sem=side_send.at[index], recv_sem=side_recv.at[index],
            device_id=device, device_id_type=MESH,
        )

    pair_out = [
        sideways(x_ref.at[pl.ds(b * BLOCK, BLOCK)], beside.at[pl.ds(b * PAD, BLOCK)], b, left) for b in range(2)
    ]
    turn_out = sideways(turn.at[0, pl.ds(PAD, PAD)], turn_in, 2, left)
    corner_out = sideways(corner, corner_in, 3, left)
    block_out = sideways(stack.at[PAIRS, pl.ds(0, PAD)], stack.at[0, pl.ds(0, PAD)], 4, right)
    wide_out = sideways(wide, wide_in, 5, right)

    pl.semaphore_wait(barrier, 2 * (SIDE - 1) + 2)
    for copy in pair_out:
        copy.start()

    def send(group, half, axis, step, source, target, kind, small=0):
        pltpu.make_async_remote_copy(
            src_ref=source, dst_ref=target, send_sem=send_sem.at[group, half, small],
            recv_sem=recv_sem.at[group, half, kind], device_id=movers[half][axis](step), device_id_type=MESH,
        ).start()

    def arrived(like, group, half, kind):
        pltpu.make_async_copy(like, like, recv_sem.at[group, half, kind]).wait()

    def chunk_of(ref, group, half, step):
        return ref.at[group, half * SIDE + ring(places[half][0], step), pl.ds(0, CHUNK)]

    def spread(group, half):
        send(group, half, 0, 2 * tie, chunk_of(part, group, half, 4), relay_in.at[group, half, 2], 0)
        for slot, step in enumerate((1, -1)):
            send(group, half, 0, step, chunk_of(part, group, half, 3 * step), relay_in.at[group, half, slot], 0)
        for slot, step in enumerate((1, -1)):
            send(group, half, 0, step, chunk_of(part, group, half, step), final_in.at[group, half, slot], 1)

    def relay(group, half):
        arrived(relay_in.at[group, half], group, half, 0)
        for slot, step in enumerate((1, -1)):
            here = chunk_of(part, group, half, 2 * step)[...] + relay_in[group, half, slot]
            relay_out[group, half, slot] = here + jnp.where(tie == step, relay_in[group, half, 2], 0.0)
            send(group, half, 0, 2 * step, relay_out.at[group, half, slot], final_in.at[group, half, 2 + slot], 1)

    def cross(group, half):
        arrived(final_in.at[group, half], group, half, 1)
        total = chunk_of(part, group, half, 0)[...]
        for slot in range(4):
            total = total + final_in[group, half, slot]
        middle[group, half, pl.ds(0, SIDE - 1)] = total.reshape(SIDE - 1, TILE, PAD)
        place = places[half][1]
        for step in FAR_FIRST:
            send(
                group, half, 1, step, middle.at[group, half, ring(place, step)], tiles.at[group, half, place], 2, 1
            )
        tiles[group, half, place] = middle[group, half, place]

    def back(group, half):
        arrived(tiles.at[group, half, pl.ds(0, SIDE - 1)], group, half, 2)
        total = tiles[group, half, 0]
        for i in range(1, SIDE):
            total = total + tiles[group, half, i]
        first, second = places[half]
        here = full.at[group, half * SIDE + first, pl.ds(pl.multiple_of(second * TILE, TILE), TILE)]
        here[...] = total
        for step in FAR_FIRST:
            send(group, half, 1, step, here, here, 3, 1)

    def share(group, half):
        arrived(tiles.at[group, half, pl.ds(0, SIDE - 1)], group, half, 3)
        here = chunk_of(full, group, half, 0)
        for step in (2, -2):
            send(group, half, 0, step, here, here, 4)
        for step in (1, -1):
            send(group, half, 0, step, here, here, 5)

    def pass_on(group, half):
        arrived(final_in.at[group, half, pl.ds(0, 2)], group, half, 4)
        here = chunk_of(full, group, half, -2 * tie)
        send(group, half, 0, 2 * tie, here, here, 5)
        for step in (1, -1):
            here = chunk_of(full, group, half, -2 * step)
            send(group, half, 0, step, here, here, 5)

    def complete(group, half):
        arrived(full.at[group, pl.ds(0, 5), pl.ds(0, CHUNK)], group, half, 5)

    def put(group, chunk, x):
        part[group, pl.ds(chunk, 2)] = x[:BLOCK].reshape(2, CHUNK, PAD)

    def take(group, chunk):
        return full[group, pl.ds(chunk, 2), pl.ds(0, CHUNK)].reshape(BLOCK, PAD)

    firsts, lasts, turnings = {}, {}, {}

    def gram_products(half):
        for k in (2 * half, 2 * half + 1):
            loads[2 * k].wait()
            loads[2 * k + 1].wait()
            pair = own[k]
            gram = dot_nt(pair, pair)
            put(0, 4 * k, packed(gram[:PAD, :PAD], gram[PAD:, PAD:]))
            put(0, 4 * k + 2, gram[:PAD, PAD:])
        spread(0, half)

    def cross_products(k):
        group, half = CROSS_PLACE[k]
        if k == PAIRS - 1:
            for copy in pair_out:
                copy.wait_recv()
        gram = dot_nt(own[k], own[k + 1] if k < PAIRS - 1 else beside[...])
        put(group, half * SIDE, gram[:PAD, :PAD])
        put(group, half * SIDE + 2, gram[:PAD, PAD:])
        put(group, half * SIDE + 4, gram[PAD:, :PAD])
        put(group, half * SIDE + 6, gram[PAD:, PAD:])
        spread(group, half)

    def first_turnings():
        for k in range(PAIRS):
            first, last = unpacked(take(0, 4 * k))
            between = padded(take(0, 4 * k + 2))
            grams[k] = square_of(first, between, between.T, last)
        for k in range(PAIRS):
            turn[k] = turning_transposed(grams[k])
        turn_out.start()

    def first_update(k):
        updated = dot(turn[k], own[k]).astype(jnp.bfloat16)
        stack[k + 1, pl.ds(0, PAD)] = updated[:PAD]
        stack[k, pl.ds(PAD, PAD)] = updated[PAD:]

    def turned_grams():
        for k in range(PAIRS):
            firsts[k] = both_sides(turn[k, pl.ds(0, PAD)], grams[k], turn[k, pl.ds(0, PAD)])
            lasts[k] = both_sides(turn[k, pl.ds(PAD, PAD)], grams[k], turn[k, pl.ds(PAD, PAD)])
        corner[...] = lasts[0]
        first_update(PAIRS - 1)
        corner_out.start()
        block_out.start()

    def first_updates():
        for k in range(PAIRS - 1):
            first_update(k)

    def update_beside():
        stack[PAIRS, pl.ds(PAD, PAD)] = dot(turn_in[...], beside[...]).astype(jnp.bfloat16)

    def second_turnings(*pairs):
        if PAIRS - 1 in pairs:
            turn_out.wait_recv()
            corner_out.wait_recv()
        between = {}
        for k in pairs:
            group, half = CROSS_PLACE[k]
            cross_gram = square_of(*[padded(take(group, half * SIDE + 2 * i)) for i in range(4)])
            other = turn[k + 1, pl.ds(PAD, PAD)] if k < PAIRS - 1 else turn_in[...]
            between[k] = both_sides(turn[k, pl.ds(0, PAD)], cross_gram, other)
        for k in pairs:
            last = lasts[k + 1] if k < PAIRS - 1 else corner_in[...]
            turnings[k] = turning_transposed(square_of(firsts[k], between[k], between[k].T, last))
        if PAIRS - 1 in pairs:
            wide[...] = turnings[PAIRS - 1][:PAD]
            wide_out.start()
    def second_update(k):
        updated = dot(turnings[k], stack[k + 1]).astype(jnp.bfloat16)
        if k < PAIRS - 1:
            o_ref[pl.ds((2 * k + 1) * BLOCK, BLOCK)] = updated[PAD : PAD + BLOCK]
            o_ref[pl.ds((2 * k + 2) * BLOCK, BLOCK)] = updated[:BLOCK]
        else:
            o_ref[pl.ds((2 * k + 1) * BLOCK, BLOCK)] = jnp.where(c == col_count - 1, stack[PAIRS, pl.ds(0, BLOCK)], updated[PAD : PAD + BLOCK])

    def first_block():
        block_out.wait_recv()
        wide_out.wait_recv()
        updated = dot(wide_in[...], stack[0]).astype(jnp.bfloat16)[:BLOCK]
        o_ref[pl.ds(0, BLOCK)] = jnp.where(c == 0, stack[0, pl.ds(PAD, BLOCK)], updated)

    plan = [(0, gram_products, 0), (0, gram_products, 1)]
    plan += [(LAG, cross_products, k) for k in CROSS_ORDER]
    units = [(0, 0), (0, 1)] + [CROSS_PLACE[k] for k in CROSS_ORDER]
    for i, unit in enumerate(units):
        for j, stage in enumerate((relay, cross, back, share, pass_on, complete)):
            plan.append(((j + 1) * STAGE + (LAG if i >= 2 else 0), stage, *unit))
    plan.append((TURN, first_turnings))
    plan.append((TURN, turned_grams))
    plan.append((100, second_turnings, *CROSS_ORDER))
    plan.append((100, first_updates))
    plan.append((100, update_beside))
    plan += [(100, second_update, k) for k in range(PAIRS)]
    plan.append((100, first_block))
    for _, step, *where in sorted(plan, key=lambda entry: entry[0]):
        step(*where)

    for copy in pair_out + [turn_out, corner_out, block_out, wide_out]:
        copy.wait_send()
    for group in range(GROUPS):
        for half in range(2):
            for small, like in enumerate((full.at[group, pl.ds(0, 14), pl.ds(0, CHUNK)], part.at[group, pl.ds(0, 2)])):
                pltpu.make_async_copy(like, like, send_sem.at[group, half, small]).wait()


def shards(weight_delta):
    width = weight_delta.shape[1]
    chunks = lambda count: pltpu.VMEM((GROUPS, 2, count, CHUNK, PAD), f32)
    f32, bf16 = jnp.float32, jnp.bfloat16
    return pl.pallas_call(
        kernel,
        out_shape=pltpu.VMEM(weight_delta.shape, bf16),
        in_specs=[pl.BlockSpec(memory_space=pl.ANY)],
        out_specs=pl.BlockSpec(memory_space=pltpu.VMEM),
        scratch_shapes=[
            pltpu.VMEM((PAIRS, 2 * PAD, width), bf16),
            pltpu.VMEM((2 * PAD, width), bf16),
            pltpu.VMEM((GROUPS, 2 * SIDE, CHUNK, PAD), f32),
            chunks(3),
            chunks(2),
            chunks(4),
            pltpu.VMEM((GROUPS, 2, SIDE, TILE, PAD), f32),
            pltpu.VMEM((GROUPS, 2, SIDE, TILE, PAD), f32),
            pltpu.VMEM((GROUPS, 2 * SIDE, SIDE * TILE, PAD), f32),
            pltpu.VMEM((PAIRS, 2 * PAD, 2 * PAD), f32),
            pltpu.VMEM((PAIRS, 2 * PAD, 2 * PAD), bf16),
            pltpu.VMEM((PAIRS + 1, 2 * PAD, width), bf16),
            pltpu.VMEM((PAD, PAD), f32),
            pltpu.VMEM((PAD, PAD), f32),
            pltpu.VMEM((PAD, 2 * PAD), bf16),
            pltpu.VMEM((PAD, 2 * PAD), bf16),
            pltpu.VMEM((PAD, 2 * PAD), bf16),
            pltpu.SemaphoreType.DMA((2 * PAIRS,)),
            pltpu.SemaphoreType.DMA((GROUPS, 2, 2)),
            pltpu.SemaphoreType.DMA((GROUPS, 2, 6)),
            pltpu.SemaphoreType.DMA((6,)),
            pltpu.SemaphoreType.DMA((6,)),
        ],
        compiler_params=pltpu.CompilerParams(
            collective_id=0, has_side_effects=True, vmem_limit_bytes=58 * 2**20
        ),
    )(weight_delta)


def solution(mesh):
    return jax.shard_map(
        shards, mesh=mesh, in_specs=(P("col", "row"),), out_specs=P("col", "row"), check_vma=False
    )
```

time: 70.2 us -> 56.1 us (0.80)
  the two profiles are of different devices: /device:TPU:1 before, /device:TPU:8 now
where the time goes in v2:
time: 56.1 us; the launch traced here: 56 us
  Pallas kernels  55.1 us (98%)
  local copies, waits for them, and re-layouts  0.93 us (2%)
    pallas_call x1, Pallas kernels, shards(): pl.pallas_call(kernel, out_shape=pltpu.VMEM(weight_delta.shape, bf16), in...  55.1 us

profile of v2, /device:TPU:8, one launch (start us, length us, event | category | flops | bytes accessed | tf_op | source)
XLA Modules:
  0.0 56.0 jit_solution(10150490109862001119)
XLA Ops:
  0.0 55.1 %shard_map.17 = bf16[896,512]{1,0:T(8,128)(2,1)S(1)} custom-call(bf16[896,512]{1,0:T(8,128)(2,1)} %x_ref.1), custom_call_target="tpu_custom_call" | custom-call | tf_op jit(solution)/shard_map/pallas_call | solution.py:353
  55.1 0.9 %copy.3 = bf16[896,512]{1,0:T(8,128)(2,1)} copy(bf16[896,512]{1,0:T(8,128)(2,1)S(1)} %shard_map.17) | data formatting | bytes 1835008

commit v3 on v2

--- a/solution.py
+++ b/solution.py
@@ -16,8 +16,8 @@
 GROUPS = 3
 EPS = 1e-6
 STAGE, LAG, TURN = 10, 5, 60.5
-CROSS_ORDER = (0, 3, 1, 2)
-CROSS_PLACE = {0: (1, 0), 3: (1, 1), 1: (2, 0), 2: (2, 1)}
+CROSS_ORDER = (0, 1, 3, 2)
+CROSS_PLACE = {0: (1, 0), 1: (1, 1), 3: (2, 0), 2: (2, 1)}
 MESH = pl.DeviceIdType.MESH
 FAR_FIRST = (4, 3, 5, 2, 6, 1, 7)
 
@@ -159,10 +159,6 @@
     block_out = sideways(stack.at[PAIRS, pl.ds(0, PAD)], stack.at[0, pl.ds(0, PAD)], 4, right)
     wide_out = sideways(wide, wide_in, 5, right)
 
-    pl.semaphore_wait(barrier, 2 * (SIDE - 1) + 2)
-    for copy in pair_out:
-        copy.start()
-
     def send(group, half, axis, step, source, target, kind, small=0):
         pltpu.make_async_remote_copy(
             src_ref=source, dst_ref=target, send_sem=send_sem.at[group, half, small],
@@ -240,15 +236,21 @@
 
     firsts, lasts, turnings = {}, {}, {}
 
-    def gram_products(half):
-        for k in (2 * half, 2 * half + 1):
+    def gram_products():
+        for k in range(PAIRS):
             loads[2 * k].wait()
             loads[2 * k + 1].wait()
             pair = own[k]
             gram = dot_nt(pair, pair)
             put(0, 4 * k, packed(gram[:PAD, :PAD], gram[PAD:, PAD:]))
             put(0, 4 * k + 2, gram[:PAD, PAD:])
-        spread(0, half)
+
+    def begin():
+        pl.semaphore_wait(barrier, 2 * (SIDE - 1) + 2)
+        for copy in pair_out:
+            copy.start()
+        for half in range(2):
+            spread(0, half)
 
     def cross_products(k):
         group, half = CROSS_PLACE[k]
@@ -262,28 +264,32 @@
         put(group, half * SIDE + 6, gram[PAD:, PAD:])
         spread(group, half)
 
-    def first_turnings():
-        for k in range(PAIRS):
+    def first_turnings(*pairs):
+        for k in pairs:
             first, last = unpacked(take(0, 4 * k))
             between = padded(take(0, 4 * k + 2))
             grams[k] = square_of(first, between, between.T, last)
-        for k in range(PAIRS):
+        for k in pairs:
             turn[k] = turning_transposed(grams[k])
-        turn_out.start()
+        if 0 in pairs:
+            turn_out.start()
 
     def first_update(k):
         updated = dot(turn[k], own[k]).astype(jnp.bfloat16)
         stack[k + 1, pl.ds(0, PAD)] = updated[:PAD]
         stack[k, pl.ds(PAD, PAD)] = updated[PAD:]
 
-    def turned_grams():
-        for k in range(PAIRS):
+    def turned_grams(*pairs):
+        for k in pairs:
+            lasts[k] = both_sides(turn[k, pl.ds(PAD, PAD)], grams[k], turn[k, pl.ds(PAD, PAD)])
+        if 0 in pairs:
+            corner[...] = lasts[0]
+            corner_out.start()
+        for k in pairs:
             firsts[k] = both_sides(turn[k, pl.ds(0, PAD)], grams[k], turn[k, pl.ds(0, PAD)])
-            lasts[k] = both_sides(turn[k, pl.ds(PAD, PAD)], grams[k], turn[k, pl.ds(PAD, PAD)])
-        corner[...] = lasts[0]
-        first_update(PAIRS - 1)
-        corner_out.start()
-        block_out.start()
+        if PAIRS - 1 in pairs:
+            first_update(PAIRS - 1)
+            block_out.start()
 
     def first_updates():
         for k in range(PAIRS - 1):
@@ -322,19 +328,24 @@
         updated = dot(wide_in[...], stack[0]).astype(jnp.bfloat16)[:BLOCK]
         o_ref[pl.ds(0, BLOCK)] = jnp.where(c == 0, stack[0, pl.ds(PAD, BLOCK)], updated)
 
-    plan = [(0, gram_products, 0), (0, gram_products, 1)]
+    plan = [(0, gram_products), (0, begin)]
     plan += [(LAG, cross_products, k) for k in CROSS_ORDER]
     units = [(0, 0), (0, 1)] + [CROSS_PLACE[k] for k in CROSS_ORDER]
     for i, unit in enumerate(units):
         for j, stage in enumerate((relay, cross, back, share, pass_on, complete)):
             plan.append(((j + 1) * STAGE + (LAG if i >= 2 else 0), stage, *unit))
-    plan.append((TURN, first_turnings))
-    plan.append((TURN, turned_grams))
-    plan.append((100, second_turnings, *CROSS_ORDER))
+    plan.append((54.9, complete, 0, 0))
+    plan.append((54.9, first_turnings, 0))
+    plan.append((54.9, turned_grams, 0))
+    plan.append((TURN, first_turnings, 1, 2, 3))
+    plan.append((TURN, turned_grams, 1, 2, 3))
+    plan.append((100, second_turnings, 3))
+    plan.append((100, second_turnings, 0, 1, 2))
     plan.append((100, first_updates))
     plan.append((100, update_beside))
     plan += [(100, second_update, k) for k in range(PAIRS)]
     plan.append((100, first_block))
+    plan.remove((6 * STAGE, complete, 0, 0))
     for _, step, *where in sorted(plan, key=lambda entry: entry[0]):
         step(*where)
 

time: 56.1 us -> 54.3 us (0.968)
  the two profiles are of different devices: /device:TPU:8 before, /device:TPU:1 now
where the time goes in v3:
time: 54.3 us; the launch traced here: 54.1 us
  Pallas kernels  53.2 us (98%)
  local copies, waits for them, and re-layouts  0.93 us (2%)
    pallas_call x1, Pallas kernels, shards(): pl.pallas_call(kernel, out_shape=pltpu.VMEM(weight_delta.shape, bf16), in...  53.2 us

profile of v3, /device:TPU:1, one launch (start us, length us, event | category | flops | bytes accessed | tf_op | source)
XLA Modules:
  0.0 54.1 jit_solution(7244738431898501109)
XLA Ops:
  0.0 53.2 %shard_map.17 = bf16[896,512]{1,0:T(8,128)(2,1)S(1)} custom-call(bf16[896,512]{1,0:T(8,128)(2,1)} %x_ref.1), custom_call_target="tpu_custom_call" | custom-call | tf_op jit(solution)/shard_map/pallas_call | solution.py:364
  53.2 0.9 %copy.3 = bf16[896,512]{1,0:T(8,128)(2,1)} copy(bf16[896,512]{1,0:T(8,128)(2,1)S(1)} %shard_map.17) | data formatting | bytes 1835008

commit v4 on v3

--- a/solution.py
+++ b/solution.py
@@ -12,12 +12,15 @@
 PAIRS = 4
 SIDE = 8
 CHUNK = 56
+SHORT = 48
+STRIP = 16
 TILE = 8
 GROUPS = 3
 EPS = 1e-6
 STAGE, LAG, TURN = 10, 5, 60.5
-CROSS_ORDER = (0, 1, 3, 2)
-CROSS_PLACE = {0: (1, 0), 1: (1, 1), 3: (2, 0), 2: (2, 1)}
+CROSS_ORDER = (0, 3, 1, 2)
+CROSS_PLACE = {0: (1, 0), 3: (1, 1), 1: (2, 0), 2: (2, 1)}
+CHUNK_ROWS = {(0, 0): CHUNK, (0, 1): CHUNK, (1, 0): SHORT, (1, 1): CHUNK, (2, 0): SHORT, (2, 1): SHORT}
 MESH = pl.DeviceIdType.MESH
 FAR_FIRST = (4, 3, 5, 2, 6, 1, 7)
 
@@ -95,6 +98,32 @@
     return first, last
 
 
+def lanes(rows):
+    return lax.broadcasted_iota(jnp.int32, (rows, PAD), 1)
+
+
+def folded(x):
+    quarters = [x[i : i + BLOCK, j : j + PAD] for i in (0, PAD) for j in (0, PAD)]
+    kept = jnp.concatenate(quarters[:3] + [quarters[3][:SHORT]], axis=0)
+    lower = quarters[3][SHORT:]
+    strips = jnp.concatenate([pltpu.roll(lower, BLOCK - STRIP * i, 1) for i in range(BLOCK // STRIP)], axis=0)
+    count = kept.shape[0]
+    return jnp.where(lanes(count) < BLOCK, kept, strips[:count]), strips[count:]
+
+
+def unfolded(kept, extra):
+    strips = jnp.concatenate([kept, extra], axis=0)
+    height = BLOCK - SHORT
+    lane = lanes(height)
+    lower = jnp.zeros((height, PAD), jnp.float32)
+    for i in range(BLOCK // STRIP):
+        moved = pltpu.roll(strips[i * height : (i + 1) * height], STRIP * (i + 1), 1)
+        lower = jnp.where((lane >= STRIP * i) & (lane < STRIP * (i + 1)), moved, lower)
+    kept = jnp.where(lanes(kept.shape[0]) < BLOCK, kept, 0.0)
+    quarters = [kept[i * BLOCK : (i + 1) * BLOCK] for i in range(3)]
+    return quarters + [jnp.concatenate([kept[3 * BLOCK :], lower], axis=0)]
+
+
 def square_of(a, b, c, d):
     return jnp.concatenate([jnp.concatenate([a, b], axis=1), jnp.concatenate([c, d], axis=1)], axis=0)
 
@@ -143,7 +172,8 @@
             own[k, pl.ds(lower, PAD - BLOCK)] = gap
     for group in range(GROUPS):
         for half in range(2):
-            middle[group, half, SIDE - 1] = jnp.zeros((TILE, PAD), jnp.float32)
+            for tile in range(CHUNK_ROWS[group, half] // TILE, SIDE):
+                middle[group, half, tile] = jnp.zeros((TILE, PAD), jnp.float32)
 
     def sideways(source, target, index, device):
         return pltpu.make_async_remote_copy(
@@ -169,28 +199,38 @@
         pltpu.make_async_copy(like, like, recv_sem.at[group, half, kind]).wait()
 
     def chunk_of(ref, group, half, step):
-        return ref.at[group, half * SIDE + ring(places[half][0], step), pl.ds(0, CHUNK)]
+        return ref.at[group, half * SIDE + ring(places[half][0], step), pl.ds(0, CHUNK_ROWS[group, half])]
+
+    def slot_of(ref, group, half, slot):
+        return ref.at[group, half, slot, pl.ds(0, CHUNK_ROWS[group, half])]
+
+    def slots_of(ref, group, half, count):
+        return ref.at[group, half, pl.ds(0, count), pl.ds(0, CHUNK_ROWS[group, half])]
 
     def spread(group, half):
-        send(group, half, 0, 2 * tie, chunk_of(part, group, half, 4), relay_in.at[group, half, 2], 0)
+        send(group, half, 0, 2 * tie, chunk_of(part, group, half, 4), slot_of(relay_in, group, half, 2), 0)
         for slot, step in enumerate((1, -1)):
-            send(group, half, 0, step, chunk_of(part, group, half, 3 * step), relay_in.at[group, half, slot], 0)
+            send(group, half, 0, step, chunk_of(part, group, half, 3 * step), slot_of(relay_in, group, half, slot), 0)
+
+    def spread_near(group, half):
         for slot, step in enumerate((1, -1)):
-            send(group, half, 0, step, chunk_of(part, group, half, step), final_in.at[group, half, slot], 1)
+            send(group, half, 0, step, chunk_of(part, group, half, step), slot_of(final_in, group, half, slot), 1)
 
     def relay(group, half):
-        arrived(relay_in.at[group, half], group, half, 0)
+        arrived(slots_of(relay_in, group, half, 3), group, half, 0)
         for slot, step in enumerate((1, -1)):
-            here = chunk_of(part, group, half, 2 * step)[...] + relay_in[group, half, slot]
-            relay_out[group, half, slot] = here + jnp.where(tie == step, relay_in[group, half, 2], 0.0)
-            send(group, half, 0, 2 * step, relay_out.at[group, half, slot], final_in.at[group, half, 2 + slot], 1)
+            here = chunk_of(part, group, half, 2 * step)[...] + slot_of(relay_in, group, half, slot)[...]
+            out = slot_of(relay_out, group, half, slot)
+            out[...] = here + jnp.where(tie == step, slot_of(relay_in, group, half, 2)[...], 0.0)
+            send(group, half, 0, 2 * step, out, slot_of(final_in, group, half, 2 + slot), 1)
 
     def cross(group, half):
-        arrived(final_in.at[group, half], group, half, 1)
+        arrived(slots_of(final_in, group, half, 4), group, half, 1)
         total = chunk_of(part, group, half, 0)[...]
         for slot in range(4):
-            total = total + final_in[group, half, slot]
-        middle[group, half, pl.ds(0, SIDE - 1)] = total.reshape(SIDE - 1, TILE, PAD)
+            total = total + slot_of(final_in, group, half, slot)[...]
+        count = CHUNK_ROWS[group, half] // TILE
+        middle[group, half, pl.ds(0, count)] = total.reshape(count, TILE, PAD)
         place = places[half][1]
         for step in FAR_FIRST:
             send(
@@ -214,11 +254,14 @@
         here = chunk_of(full, group, half, 0)
         for step in (2, -2):
             send(group, half, 0, step, here, here, 4)
+
+    def share_near(group, half):
+        here = chunk_of(full, group, half, 0)
         for step in (1, -1):
             send(group, half, 0, step, here, here, 5)
 
     def pass_on(group, half):
-        arrived(final_in.at[group, half, pl.ds(0, 2)], group, half, 4)
+        arrived(slots_of(final_in, group, half, 2), group, half, 4)
         here = chunk_of(full, group, half, -2 * tie)
         send(group, half, 0, 2 * tie, here, here, 5)
         for step in (1, -1):
@@ -226,7 +269,7 @@
             send(group, half, 0, step, here, here, 5)
 
     def complete(group, half):
-        arrived(full.at[group, pl.ds(0, 5), pl.ds(0, CHUNK)], group, half, 5)
+        arrived(full.at[group, pl.ds(0, 5), pl.ds(0, CHUNK_ROWS[group, half])], group, half, 5)
 
     def put(group, chunk, x):
         part[group, pl.ds(chunk, 2)] = x[:BLOCK].reshape(2, CHUNK, PAD)
@@ -237,13 +280,21 @@
     firsts, lasts, turnings = {}, {}, {}
 
     def gram_products():
+        for copy in loads:
+            copy.wait()
         for k in range(PAIRS):
-            loads[2 * k].wait()
-            loads[2 * k + 1].wait()
             pair = own[k]
             gram = dot_nt(pair, pair)
             put(0, 4 * k, packed(gram[:PAD, :PAD], gram[PAD:, PAD:]))
-            put(0, 4 * k + 2, gram[:PAD, PAD:])
+            between = gram[:BLOCK, PAD:]
+            if k < PAIRS - 1:
+                kept, extra = folded(dot_nt(pair, own[k + 1]))
+                group, half = CROSS_PLACE[k]
+                part[group, pl.ds(half * SIDE, SIDE), pl.ds(0, SHORT)] = kept.reshape(SIDE, SHORT, PAD)
+                rows = extra.shape[0]
+                beginning = jnp.where(lanes(rows) < BLOCK, between[:rows], extra)
+                between = jnp.concatenate([beginning, between[rows:]], axis=0)
+            put(0, 4 * k + 2, between)
 
     def begin():
         pl.semaphore_wait(barrier, 2 * (SIDE - 1) + 2)
@@ -257,17 +308,25 @@
         if k == PAIRS - 1:
             for copy in pair_out:
                 copy.wait_recv()
-        gram = dot_nt(own[k], own[k + 1] if k < PAIRS - 1 else beside[...])
-        put(group, half * SIDE, gram[:PAD, :PAD])
-        put(group, half * SIDE + 2, gram[:PAD, PAD:])
-        put(group, half * SIDE + 4, gram[PAD:, :PAD])
-        put(group, half * SIDE + 6, gram[PAD:, PAD:])
+            gram = dot_nt(own[k], beside[...])
+            put(group, half * SIDE, gram[:PAD, :PAD])
+            put(group, half * SIDE + 2, gram[:PAD, PAD:])
+            put(group, half * SIDE + 4, gram[PAD:, :PAD])
+            put(group, half * SIDE + 6, gram[PAD:, PAD:])
         spread(group, half)
 
+    def cross_quarters(k):
+        group, half = CROSS_PLACE[k]
+        if k == PAIRS - 1:
+            return [padded(take(group, half * SIDE + 2 * i)) for i in range(4)]
+        kept = full[group, pl.ds(half * SIDE, SIDE), pl.ds(0, SHORT)].reshape(SIDE * SHORT, PAD)
+        return [padded(x) for x in unfolded(kept, take(0, 4 * k + 2)[: BLOCK - SHORT])]
+
     def first_turnings(*pairs):
         for k in pairs:
             first, last = unpacked(take(0, 4 * k))
-            between = padded(take(0, 4 * k + 2))
+            between = take(0, 4 * k + 2)
+            between = padded(jnp.where(lanes(BLOCK) < BLOCK, between, 0.0))
             grams[k] = square_of(first, between, between.T, last)
         for k in pairs:
             turn[k] = turning_transposed(grams[k])
@@ -304,8 +363,7 @@
             corner_out.wait_recv()
         between = {}
         for k in pairs:
-            group, half = CROSS_PLACE[k]
-            cross_gram = square_of(*[padded(take(group, half * SIDE + 2 * i)) for i in range(4)])
+            cross_gram = square_of(*cross_quarters(k))
             other = turn[k + 1, pl.ds(PAD, PAD)] if k < PAIRS - 1 else turn_in[...]
             between[k] = both_sides(turn[k, pl.ds(0, PAD)], cross_gram, other)
         for k in pairs:
@@ -329,7 +387,7 @@
         o_ref[pl.ds(0, BLOCK)] = jnp.where(c == 0, stack[0, pl.ds(PAD, BLOCK)], updated)
 
     plan = [(0, gram_products), (0, begin)]
-    plan += [(LAG, cross_products, k) for k in CROSS_ORDER]
+    plan += [(LAG, cross_products, k) for k in (0, 1, 3, 2)]
     units = [(0, 0), (0, 1)] + [CROSS_PLACE[k] for k in CROSS_ORDER]
     for i, unit in enumerate(units):
         for j, stage in enumerate((relay, cross, back, share, pass_on, complete)):
@@ -337,15 +395,19 @@
     plan.append((54.9, complete, 0, 0))
     plan.append((54.9, first_turnings, 0))
     plan.append((54.9, turned_grams, 0))
+    plan += [(LAG + 0.5, spread_near, *unit) for unit in units]
+    plan += [(4 * STAGE + LAG + 0.5, share_near, *unit) for unit in units]
     plan.append((TURN, first_turnings, 1, 2, 3))
     plan.append((TURN, turned_grams, 1, 2, 3))
-    plan.append((100, second_turnings, 3))
+    plan.append((64.5, complete, *CROSS_PLACE[3]))
+    plan.append((64.5, second_turnings, 3))
     plan.append((100, second_turnings, 0, 1, 2))
     plan.append((100, first_updates))
     plan.append((100, update_beside))
     plan += [(100, second_update, k) for k in range(PAIRS)]
     plan.append((100, first_block))
     plan.remove((6 * STAGE, complete, 0, 0))
+    plan.remove((6 * STAGE + LAG, complete, *CROSS_PLACE[3]))
     for _, step, *where in sorted(plan, key=lambda entry: entry[0]):
         step(*where)
 
@@ -353,7 +415,7 @@
         copy.wait_send()
     for group in range(GROUPS):
         for half in range(2):
-            for small, like in enumerate((full.at[group, pl.ds(0, 14), pl.ds(0, CHUNK)], part.at[group, pl.ds(0, 2)])):
+            for small, like in enumerate((full.at[group, pl.ds(0, 14), pl.ds(0, CHUNK_ROWS[group, half])], part.at[group, pl.ds(0, 2)])):
                 pltpu.make_async_copy(like, like, send_sem.at[group, half, small]).wait()
 
 

time: 54.3 us -> 53.4 us (0.983)
  Pallas kernels: 53.2 us -> 52 us
    pallas_call x1, Pallas kernels: 53.2 us -> 52 us  [shards(): pl.pallas_call(kernel, out_shape=pltpu.VMEM(weight_delta.shape, bf16), in...]
where the time goes in v4:
time: 53.4 us; the launch traced here: 52.9 us
  Pallas kernels  52 us (97%)
  local copies, waits for them, and re-layouts  0.93 us (2%)
    pallas_call x1, Pallas kernels, shards(): pl.pallas_call(kernel, out_shape=pltpu.VMEM(weight_delta.shape, bf16), in...  52 us

profile of v4, /device:TPU:1, one launch (start us, length us, event | category | flops | bytes accessed | tf_op | source)
XLA Modules:
  0.0 52.9 jit_solution(9649313064006340818)
XLA Ops:
  0.0 52.0 %shard_map.17 = bf16[896,512]{1,0:T(8,128)(2,1)S(1)} custom-call(bf16[896,512]{1,0:T(8,128)(2,1)} %x_ref.1), custom_call_target="tpu_custom_call" | custom-call | tf_op jit(solution)/shard_map/pallas_call | solution.py:426
  52.0 0.9 %copy.3 = bf16[896,512]{1,0:T(8,128)(2,1)} copy(bf16[896,512]{1,0:T(8,128)(2,1)S(1)} %shard_map.17) | data formatting | bytes 1835008

commit v5 on v4

--- a/solution.py
+++ b/solution.py
@@ -23,6 +23,7 @@
 CHUNK_ROWS = {(0, 0): CHUNK, (0, 1): CHUNK, (1, 0): SHORT, (1, 1): CHUNK, (2, 0): SHORT, (2, 1): SHORT}
 MESH = pl.DeviceIdType.MESH
 FAR_FIRST = (4, 3, 5, 2, 6, 1, 7)
+NEAR = (1, -1, 2, -2)
 
 
 def dot(a, b):
@@ -151,7 +152,7 @@
     movers = ((along_y, along_z), (along_z, along_y))
 
     barrier = pltpu.get_barrier_semaphore()
-    for step in range(1, SIDE):
+    for step in NEAR:
         pl.semaphore_signal(barrier, inc=1, device_id=along_y(step), device_id_type=MESH)
         pl.semaphore_signal(barrier, inc=1, device_id=along_z(step), device_id_type=MESH)
     for side in (left, right):
@@ -224,8 +225,13 @@
             out[...] = here + jnp.where(tie == step, slot_of(relay_in, group, half, 2)[...], 0.0)
             send(group, half, 0, 2 * step, out, slot_of(final_in, group, half, 2 + slot), 1)
 
+    def met():
+        for half in range(2):
+            arrived(slots_of(final_in, 0, half, 4), 0, half, 1)
+
     def cross(group, half):
-        arrived(slots_of(final_in, group, half, 4), group, half, 1)
+        if group > 0:
+            arrived(slots_of(final_in, group, half, 4), group, half, 1)
         total = chunk_of(part, group, half, 0)[...]
         for slot in range(4):
             total = total + slot_of(final_in, group, half, slot)[...]
@@ -280,9 +286,9 @@
     firsts, lasts, turnings = {}, {}, {}
 
     def gram_products():
-        for copy in loads:
-            copy.wait()
         for k in range(PAIRS):
+            for b in range(2 * k + 2 if k else 0, min(2 * k + 4, 2 * PAIRS)):
+                loads[b].wait()
             pair = own[k]
             gram = dot_nt(pair, pair)
             put(0, 4 * k, packed(gram[:PAD, :PAD], gram[PAD:, PAD:]))
@@ -297,7 +303,7 @@
             put(0, 4 * k + 2, between)
 
     def begin():
-        pl.semaphore_wait(barrier, 2 * (SIDE - 1) + 2)
+        pl.semaphore_wait(barrier, 2 * len(NEAR) + 2)
         for copy in pair_out:
             copy.start()
         for half in range(2):
@@ -397,6 +403,7 @@
     plan.append((54.9, turned_grams, 0))
     plan += [(LAG + 0.5, spread_near, *unit) for unit in units]
     plan += [(4 * STAGE + LAG + 0.5, share_near, *unit) for unit in units]
+    plan.append((2 * STAGE - 0.01, met))
     plan.append((TURN, first_turnings, 1, 2, 3))
     plan.append((TURN, turned_grams, 1, 2, 3))
     plan.append((64.5, complete, *CROSS_PLACE[3]))

time: 53.4 us -> 52.8 us (0.989)
  Pallas kernels: 52 us -> 51.1 us
    pallas_call x1, Pallas kernels: 52 us -> 51.1 us  [shards(): pl.pallas_call(kernel, out_shape=pltpu.VMEM(weight_delta.shape, bf16), in...]
where the time goes in v5:
time: 52.8 us; the launch traced here: 52 us
  Pallas kernels  51.1 us (97%)
  local copies, waits for them, and re-layouts  0.93 us (2%)
    pallas_call x1, Pallas kernels, shards(): pl.pallas_call(kernel, out_shape=pltpu.VMEM(weight_delta.shape, bf16), in...  51.1 us

profile of v5, /device:TPU:1, one launch (start us, length us, event | category | flops | bytes accessed | tf_op | source)
XLA Modules:
  0.0 52.0 jit_solution(17755933887245847793)
XLA Ops:
  0.0 51.1 %shard_map.17 = bf16[896,512]{1,0:T(8,128)(2,1)S(1)} custom-call(bf16[896,512]{1,0:T(8,128)(2,1)} %x_ref.1), custom_call_target="tpu_custom_call" | custom-call | tf_op jit(solution)/shard_map/pallas_call | solution.py:433
  51.1 0.9 %copy.3 = bf16[896,512]{1,0:T(8,128)(2,1)} copy(bf16[896,512]{1,0:T(8,128)(2,1)S(1)} %shard_map.17) | data formatting | bytes 1835008

commit v6 on v5

--- a/solution.py
+++ b/solution.py
@@ -285,8 +285,8 @@
 
     firsts, lasts, turnings = {}, {}, {}
 
-    def gram_products():
-        for k in range(PAIRS):
+    def gram_products(half):
+        for k in (2 * half, 2 * half + 1):
             for b in range(2 * k + 2 if k else 0, min(2 * k + 4, 2 * PAIRS)):
                 loads[b].wait()
             pair = own[k]
@@ -306,8 +306,6 @@
         pl.semaphore_wait(barrier, 2 * len(NEAR) + 2)
         for copy in pair_out:
             copy.start()
-        for half in range(2):
-            spread(0, half)
 
     def cross_products(k):
         group, half = CROSS_PLACE[k]
@@ -392,7 +390,7 @@
         updated = dot(wide_in[...], stack[0]).astype(jnp.bfloat16)[:BLOCK]
         o_ref[pl.ds(0, BLOCK)] = jnp.where(c == 0, stack[0, pl.ds(PAD, BLOCK)], updated)
 
-    plan = [(0, gram_products), (0, begin)]
+    plan = [(0, gram_products, 0), (0, begin), (0, spread, 0, 0), (0, gram_products, 1), (0, spread, 0, 1)]
     plan += [(LAG, cross_products, k) for k in (0, 1, 3, 2)]
     units = [(0, 0), (0, 1)] + [CROSS_PLACE[k] for k in CROSS_ORDER]
     for i, unit in enumerate(units):

time: 52.8 us -> 52.7 us (level)
  no operation moved by 1% of the time
where the time goes in v6:
time: 52.7 us; the launch traced here: 52.4 us
  Pallas kernels  51.4 us (98%)
  local copies, waits for them, and re-layouts  0.93 us (2%)
    pallas_call x1, Pallas kernels, shards(): pl.pallas_call(kernel, out_shape=pltpu.VMEM(weight_delta.shape, bf16), in...  51.4 us

profile of v6, /device:TPU:1, one launch (start us, length us, event | category | flops | bytes accessed | tf_op | source)
XLA Modules:
  0.0 52.4 jit_solution(2378528095343068245)
XLA Ops:
  0.0 51.4 %shard_map.17 = bf16[896,512]{1,0:T(8,128)(2,1)S(1)} custom-call(bf16[896,512]{1,0:T(8,128)(2,1)} %x_ref.1), custom_call_target="tpu_custom_call" | custom-call | tf_op jit(solution)/shard_map/pallas_call | solution.py:431
  51.4 0.9 %copy.3 = bf16[896,512]{1,0:T(8,128)(2,1)} copy(bf16[896,512]{1,0:T(8,128)(2,1)S(1)} %shard_map.17) | data formatting | bytes 1835008
